TPU v7x, 128 devices: a whole 4x4x4 slice. The times are simulated.
128 devices in a mesh: win: 8 (over y, core), blk: 16 (over z, x).
Axes of the slice: x: 4, y: 4, z: 4, core: 2. Of those that a mesh axis runs over, the one named last changes fastest.
Arguments:
- records: bfloat16 [32, 8192, 4096], P('win', 'blk'), may hold values from -6 to 6
- active: int32 [16, 5], P('blk'), may hold values from 0 to 1, as said below
Outputs:
- summary: bfloat16 [16, 5, 8, 1024, 512], P('blk', None, 'win')
Inputs may be any that keep to these rules, and one draw needn't show every extreme that they name: active[a, s] is 1 or 0; it is 0 wherever a + s >= 16; active[a, 0] is 1 for every block; some block has all 5 entries 1.
All inputs are finite; a program needn't handle non-finite values.
Results may differ from a plain program's by a relative error of at most 0.0056.
Values may be sent and summed in bfloat16 or wider, within the bound.
A program may use at most 64 MiB of HBM per device.

v0:
```python
import math

import jax
import jax.numpy as jnp
from jax import lax
from jax.sharding import PartitionSpec as P

BINS = 256
BIN0 = 16
SLOTS = 5
BAND_BINS = 32


EPSILON = 1e-06


def passed_along(x, axis, by):
    devices = lax.axis_size(axis)
    pairs = [(i, i + by) for i in range(devices) if 0 <= i + by < devices]
    return lax.ppermute(x, axis, pairs)


def spectral_table(samples, first_bin, num_bins):
    sample_idx = jnp.arange(samples, dtype=jnp.int32)[:, None]
    bin_idx = (jnp.arange(num_bins, dtype=jnp.int32) + first_bin)[None, :]
    phase_idx = sample_idx * bin_idx % samples
    angles = phase_idx.astype(jnp.float32) * (2.0 * math.pi / samples)
    return jnp.concatenate([jnp.cos(angles), -jnp.sin(angles)], axis=1).astype(jnp.bfloat16)


def pair_summary(own_bins, partner_bins, factor):
    stations = own_bins.shape[2] // 2
    left = own_bins.reshape(-1, 2 * stations)
    right = partner_bins.reshape(-1, 2 * stations)
    products = lax.dot_general(
        left, right, (((0,), (0,)), ((), ())), preferred_element_type=jnp.float32
    )
    real_sum = products[:stations, :stations] + products[stations:, stations:]
    imag_sum = products[stations:, :stations] - products[:stations, stations:]
    band_rows = [(jnp.concatenate([real_sum, imag_sum], axis=0) * factor).astype(jnp.bfloat16)]
    return jnp.stack(band_rows)


def shards(records, active):
    window_count, stations, samples = records.shape
    basis_table = spectral_table(samples, BIN0, BINS)
    spectra = jnp.einsum("wsn,nk->wsk", records, basis_table, preferred_element_type=jnp.float32)
    power_mean = jnp.sum(spectra * spectra, axis=2, keepdims=True) / BINS
    whitened = (spectra * lax.rsqrt(power_mean + EPSILON)).astype(jnp.bfloat16)
    by_bin = jnp.transpose(whitened.reshape(window_count, stations, 2, BINS), (0, 3, 2, 1))
    by_bin = by_bin.reshape(window_count, BINS, 2 * stations)
    own_bins = lax.all_to_all(by_bin, "win", split_axis=1, concat_axis=0, tiled=True)
    inv_scale = 1.0 / math.sqrt(own_bins.shape[0] * BAND_BINS)
    slot_rows = [pair_summary(own_bins, own_bins, active[0, 0].astype(jnp.float32) * inv_scale)]
    partner_bins = own_bins
    for slot_idx in range(1, SLOTS):
        partner_bins = passed_along(own_bins, "blk", -slot_idx)
        factor = active[0, slot_idx].astype(jnp.float32) * inv_scale
        slot_rows.append(pair_summary(own_bins, partner_bins, factor))
    return jnp.stack(slot_rows)[None]


def solution(mesh):
    placed = (P("win", "blk", None), P("blk", None))
    return jax.shard_map(
        shards,
        mesh=mesh,
        in_specs=placed,
        out_specs=P("blk", None, "win", None, None),
        check_vma=False,
    )
```

profile of v0, /device:TPU:6, one launch (start us, length us, event | category | flops | bytes accessed | tf_op | source)
XLA Modules:
  0.0 263.8 jit_solution(4840630138152030998)
XLA Ops:
  0.0 18.8 %cosine_convert_fusion = (bf16[4096,256]{0,1:T(8,128)(2,1)S(1)}, bf16[4096,256]{0,1:T(8,128)(2,1)}) fusion(s32[256]{0:T(256)S(1)} %iota_add_fusion), kind=kLoop, calls=%fused_computation.13 | loop fusion | flops 17825792 | bytes 4195328 | tf_op jit(solution)/shard_map/convert
  18.8 12.5 %multiply_reduce_fusion = (f32[4,512]{1,0:T(4,128)S(1)}, f32[512,4,512]{2,0,1:T(8,128)S(1)}) fusion(bf16[4,512,4096]{2,1,0:T(8,128)(2,1)} %param.2, bf16[4096,256]{0,1:T(8,128)(2,1)} %get-tuple-element.16, bf16[4096,256]{0,1:T(8,128)(2,1)S(1)} %get-tuple-element.15), kind=kOutput, calls=%fused_computation.11 | convolution fusion | flops 8600418304 | bytes 25174016 | tf_op jit(solution)/shard_map/wsn,nk->wsk/dot_general | solution.py:47
  31.3 0.6 multiply_convert_fusion
  32.0 2.3 copy.8
  34.3 4.5 %copy.9 = bf16[4,256,1024]{2,0,1:T(4,128)(2,1)} copy(bf16[4,256,1024]{1,2,0:T(8,128)(2,1)} %bitcast.67) | data formatting | bytes 4194304 | tf_op jit(solution)/shard_map/reshape | solution.py:51
  38.8 0.0 copy-start.1
  38.8 4.6 %all-to-all-start = ((bf16[4,256,1024]{2,0,1:T(4,128)(2,1)}), bf16[4,256,1024]{2,0,1:T(4,128)(2,1)S(1)}, u32[]{:S(2)}, u32[]{:S(2)}) async-start(bf16[4,256,1024]{2,0,1:T(4,128)(2,1)} %copy.9), calls=%async_computation | async-start | bytes 4194304 | tf_op jit(solution)/shard_map/all_to_all | solution.py:52
  43.4 0.0 copy-done.1
  43.4 0.6 fusion.32
  47.1 23.5 %all-to-all-done = bf16[4,256,1024]{2,0,1:T(4,128)(2,1)S(1)} async-done(((bf16[4,256,1024]{2,0,1:T(4,128)(2,1)}), bf16[4,256,1024]{2,0,1:T(4,128)(2,1)S(1)}, u32[]{:S(2)}, u32[]{:S(2)}) %all-to-all-start) | async-done | bytes 2097184 | tf_op jit(solution)/shard_map/all_to_all | solution.py:52
  70.6 0.7 copy.11
  71.3 2.7 %collective-permute-start = (bf16[32,32,1024]{2,1,0:T(8,128)(2,1)S(1)}, bf16[32,32,1024]{2,1,0:T(8,128)(2,1)S(1)}, u32[]{:S(2)}, u32[]{:S(2)}) collective-permute-start(bf16[32,32,1024]{2,1,0:T(8,128)(2,1)S(1)} %bitcast.68), channel_id=1, source_target_pairs={{1,0},{2,1},{3,2},{4,3},{5,4},{6,5},{7,6},{8,7},{9,8},{10,9},{11,1... | collective-permute-start | bytes 6291464 | tf_op jit(solution)/shard_map/ppermute | solution.py:20
  74.1 3.0 %collective-permute-start.1 = (bf16[32,32,1024]{2,1,0:T(8,128)(2,1)S(1)}, bf16[32,32,1024]{2,1,0:T(8,128)(2,1)S(1)}, u32[]{:S(2)}, u32[]{:S(2)}) collective-permute-start(bf16[32,32,1024]{2,1,0:T(8,128)(2,1)S(1)} %bitcast.69), channel_id=1, source_target_pairs={{2,0},{3,1},{4,2},{5,3},{6,4},{7,5},{8,6},{9,7},{10,8},{11,9},{12,... | collective-permute-start | bytes 6291464 | tf_op jit(solution)/shard_map/ppermute | solution.py:20
  77.1 2.7 %convolution_bitcast_fusion = f32[1024,1024]{1,0:T(8,128)S(1)} fusion(bf16[4,8,32,1024]{3,0,2,1:T(4,128)(2,1)S(1)} %bitcast.65), kind=kOutput, calls=%fused_computation.17 | convolution fusion | flops 2147483648 | bytes 6291456 | tf_op jit(solution)/shard_map/dot_general | solution.py:35
  79.8 1.9 collective-permute-start.2
  81.7 1.5 collective-permute-start.3
  83.2 0.5 fusion.29
  83.7 0.3 fusion.19
  84.0 109.8 %collective-permute-done = bf16[32,32,1024]{2,1,0:T(8,128)(2,1)S(1)} collective-permute-done((bf16[32,32,1024]{2,1,0:T(8,128)(2,1)S(1)}, bf16[32,32,1024]{2,1,0:T(8,128)(2,1)S(1)}, u32[]{:S(2)}, u32[]{:S(2)}) %collective-permute-start) | collective-permute-done | bytes 2097184 | tf_op jit(solution)/shard_map/ppermute | solution.py:20
  193.8 2.4 fusion.33
  196.2 0.5 fusion.27
  196.7 0.0 collective-permute-done.1
  196.7 2.4 fusion.34
  199.1 0.5 fusion.25
  199.6 12.9 %collective-permute-done.2 = bf16[32,32,1024]{2,1,0:T(8,128)(2,1)S(1)} collective-permute-done((bf16[32,32,1024]{2,1,0:T(8,128)(2,1)S(1)}, bf16[32,32,1024]{2,1,0:T(8,128)(2,1)S(1)}, u32[]{:S(2)}, u32[]{:S(2)}) %collective-permute-start.2) | collective-permute-done | bytes 2097184 | tf_op jit(solution)/shard_map/ppermute | solution.py:20
  212.5 2.4 fusion.35
  214.9 0.5 fusion.23
  215.4 41.9 %collective-permute-done.3 = bf16[32,32,1024]{2,1,0:T(8,128)(2,1)S(1)} collective-permute-done((bf16[32,32,1024]{2,1,0:T(8,128)(2,1)S(1)}, bf16[32,32,1024]{2,1,0:T(8,128)(2,1)S(1)}, u32[]{:S(2)}, u32[]{:S(2)}) %collective-permute-start.3) | collective-permute-done | bytes 2097184 | tf_op jit(solution)/shard_map/ppermute | solution.py:20
  257.3 2.4 fusion.36
  259.8 0.5 fusion.21
  260.3 0.3 fusion.18
  260.5 0.3 fusion.17
  260.8 0.3 fusion.16
  261.1 0.3 fusion.15
  261.4 0.0 copy-start
  261.4 2.3 copy-done
  (2 shorter events, 0.0 us)
Async XLA Ops:
  38.8 4.6 %copy-start.1 = (s32[1,5]{1,0:T(1,128)S(1)}, s32[1,5]{1,0:T(1,128)}, u32[]{:S(2)}) copy-start(s32[1,5]{1,0:T(1,128)} %param.3) | copy-start | bytes 64
  38.8 31.8 %all-to-all-start = ((bf16[4,256,1024]{2,0,1:T(4,128)(2,1)}), bf16[4,256,1024]{2,0,1:T(4,128)(2,1)S(1)}, u32[]{:S(2)}, u32[]{:S(2)}) async-start(bf16[4,256,1024]{2,0,1:T(4,128)(2,1)} %copy.9), calls=%async_computation | async-start | bytes 4194304 | tf_op jit(solution)/shard_map/all_to_all | solution.py:52
  71.3 122.4 %collective-permute-start = (bf16[32,32,1024]{2,1,0:T(8,128)(2,1)S(1)}, bf16[32,32,1024]{2,1,0:T(8,128)(2,1)S(1)}, u32[]{:S(2)}, u32[]{:S(2)}) collective-permute-start(bf16[32,32,1024]{2,1,0:T(8,128)(2,1)S(1)} %bitcast.68), channel_id=1, source_target_pairs={{1,0},{2,1},{3,2},{4,3},{5,4},{6,5},{7,6},{8,7},{9,8},{10,9},{11,1... | collective-permute-start | bytes 6291464 | tf_op jit(solution)/shard_map/ppermute | solution.py:20
  74.1 122.6 %collective-permute-start.1 = (bf16[32,32,1024]{2,1,0:T(8,128)(2,1)S(1)}, bf16[32,32,1024]{2,1,0:T(8,128)(2,1)S(1)}, u32[]{:S(2)}, u32[]{:S(2)}) collective-permute-start(bf16[32,32,1024]{2,1,0:T(8,128)(2,1)S(1)} %bitcast.69), channel_id=1, source_target_pairs={{2,0},{3,1},{4,2},{5,3},{6,4},{7,5},{8,6},{9,7},{10,8},{11,9},{12,... | collective-permute-start | bytes 6291464 | tf_op jit(solution)/shard_map/ppermute | solution.py:20
  79.8 132.7 %collective-permute-start.2 = (bf16[32,32,1024]{2,1,0:T(8,128)(2,1)S(1)}, bf16[32,32,1024]{2,1,0:T(8,128)(2,1)S(1)}, u32[]{:S(2)}, u32[]{:S(2)}) collective-permute-start(bf16[32,32,1024]{2,1,0:T(8,128)(2,1)S(1)} %bitcast.70), channel_id=1, source_target_pairs={{3,0},{4,1},{5,2},{6,3},{7,4},{8,5},{9,6},{10,7},{11,8},{12,9},{13... | collective-permute-start | bytes 6291464 | tf_op jit(solution)/shard_map/ppermute | solution.py:20
  81.7 175.6 %collective-permute-start.3 = (bf16[32,32,1024]{2,1,0:T(8,128)(2,1)S(1)}, bf16[32,32,1024]{2,1,0:T(8,128)(2,1)S(1)}, u32[]{:S(2)}, u32[]{:S(2)}) collective-permute-start(bf16[32,32,1024]{2,1,0:T(8,128)(2,1)S(1)} %bitcast.71), channel_id=1, source_target_pairs={{4,0},{5,1},{6,2},{7,3},{8,4},{9,5},{10,6},{11,7},{12,8},{13,9},{1... | collective-permute-start | bytes 6291464 | tf_op jit(solution)/shard_map/ppermute | solution.py:20
  261.4 2.4 copy-start
where the time goes:
time: 264 us
  waiting for transfers between devices  188 us (71%)
  matrix products  24.8 us (9%)
  other arithmetic  23.3 us (9%)
  starting transfers between devices  13.7 us (5%)
  local copies, waits for them, and re-layouts  10.6 us (4%)
  between operations  3.26 us (1%)
    ppermute x4, waiting for transfers between devices, passed_along(): return lax.ppermute(x, axis, pairs)  165 us
    all_to_all x1, waiting for transfers between devices, shards(): lax.all_to_all(by_bin, 'win', split_axis=1, concat_axis=0, tiled=True)  23.5 us
    another operation x1, other arithmetic  18.8 us
    dot_general x1, matrix products, shards(): jnp.einsum('wsn,nk->wsk', records, basis_table, preferred_element_type=jn...  12.5 us
    dot_general x5, matrix products, pair_summary(): lax.dot_general(left, right, (((0,), (0,)), ((), ())), preferred_element_...  12.3 us
    ppermute x4, starting transfers between devices, passed_along(): return lax.ppermute(x, axis, pairs)  9.15 us
  transfers between devices with their start and end apart: 5, of which 4 were waited for; matrix products, arithmetic and copies ran while one was open for 5% of the time, Pallas kernels for 0%

commit v1 on v0

v1 whole, which is shorter than its diff:
```python
import functools
import math

import jax
import jax.numpy as jnp
import ml_dtypes
import numpy as np
from jax import lax
from jax.experimental import pallas as pl
from jax.experimental.pallas import tpu as pltpu
from jax.sharding import PartitionSpec as P

SAMPLES = 4096
BINS = 256
BIN0 = 16
SLOTS = 5
BAND_BINS = 32
EPSILON = 1e-06

WIN = 8
RING = 4
BLOCKS = 16
LOCAL_W = 4
ST = 512
Q = 128
K = 1024
PIECES = 32
LAG = 3

MESH = pl.DeviceIdType.MESH
F32 = jnp.float32
BF16 = jnp.bfloat16

OWN, UP4, UP1, UP3 = 0, 1, 2, 3


def spectral_table():
    phase = (np.arange(BINS)[:, None] + BIN0) * np.arange(SAMPLES)[None, :] % SAMPLES
    angles = phase.astype(np.float32) * np.float32(2.0 * math.pi / SAMPLES)
    angles = angles.astype(np.float64)
    return np.concatenate([np.cos(angles), -np.sin(angles)]).astype(np.float32).astype(ml_dtypes.bfloat16)


def kernel(active, rec, table, out, tab, rbuf, wh, blk, a2, lt, rp, rv, ost,
           tab_sem, rec_sem, aa_send, aa_recv, z_send, z_recv, m_send, m_recv, p_send, p_recv,
           a2_send, a2_recv, ret_send, ret_recv, out_sem):
    me = lax.axis_index("win")
    b = lax.axis_index("blk")
    z, x = b // RING, b % RING

    def peer(i):
        return (lax.rem(me + i, WIN), b)

    def at(dz, dx):
        return (me, lax.rem(z + dz + RING, RING) * RING + lax.rem(x + dx + RING, RING))

    nxt = (me, lax.rem(b + 1, BLOCKS))
    prv = (me, lax.rem(b + BLOCKS - 1, BLOCKS))

    barrier = pltpu.get_barrier_semaphore()
    for i in range(1, WIN):
        pl.semaphore_signal(barrier, inc=1, device_id=peer(i), device_id_type=MESH)
    for dev in (at(-1, 0), at(1, 0), at(0, -1), at(0, 1), nxt, prv):
        pl.semaphore_signal(barrier, inc=1, device_id=dev, device_id_type=MESH)

    pltpu.make_async_copy(table, tab, tab_sem).start()
    for sc in range(8):
        h, w = sc // LOCAL_W, sc % LOCAL_W
        pltpu.make_async_copy(rec.at[w, pl.ds(h * 2 * Q, 2 * Q), :], rbuf.at[sc], rec_sem.at[sc]).start()

    pltpu.make_async_copy(table, tab, tab_sem).wait()
    pl.semaphore_wait(barrier, WIN - 1 + 6)

    def transform(sc):
        h, w = sc // LOCAL_W, sc % LOCAL_W
        pltpu.make_async_copy(rbuf.at[sc], rbuf.at[sc], rec_sem.at[sc]).wait()
        spectra = lax.dot_general(tab[...], rbuf[sc], (((1,), (1,)), ((), ())), preferred_element_type=F32)
        power = jnp.sum(spectra * spectra, axis=0, keepdims=True) / BINS
        white = (spectra * lax.rsqrt(power + EPSILON)).astype(BF16)
        for q in range(WIN):
            for ri in range(2):
                for qt in range(2):
                    wh[sc, q, qt, ri] = white[ri * BINS + q * BAND_BINS:ri * BINS + (q + 1) * BAND_BINS,
                                              qt * Q:(qt + 1) * Q]
        row = pl.multiple_of((w * WIN + me) * BAND_BINS, BAND_BINS)

        @pl.loop(1, WIN)
        def _(i):
            to = peer(i)
            pltpu.make_async_remote_copy(
                src_ref=wh.at[sc, to[0]],
                dst_ref=blk.at[OWN, pl.ds(h * 2, 2), :, pl.ds(row, BAND_BINS), :],
                send_sem=aa_send.at[sc], recv_sem=aa_recv.at[sc], device_id=to, device_id_type=MESH,
            ).start()

        for qt in range(2):
            for ri in range(2):
                blk[OWN, h * 2 + qt, ri, pl.ds(row, BAND_BINS), :] = wh[sc, me, qt, ri]

    def piece(block, j):
        return blk.at[block, j // 8, j % 2, pl.ds((j // 2) % 4 * 256, 256), :]

    m_src = jnp.where(x >= 1, OWN, UP4)
    p_src = jnp.where(x <= 2, UP4, OWN)

    def wait_bytes(ref, sem):
        pltpu.make_async_copy(ref, ref, sem).wait()

    def tick(k):
        if k < PIECES:
            if k % 2 == 0 and (k // 8) % 2 == 0:
                sc = k // 16 * 4 + (k // 2) % 4
                wait_bytes(wh.at[sc, pl.ds(0, WIN - 1)], aa_recv.at[sc])
            pltpu.make_async_remote_copy(
                src_ref=piece(OWN, k), dst_ref=piece(UP4, k),
                send_sem=z_send, recv_sem=z_recv.at[k], device_id=at(-1, 0), device_id_type=MESH).start()
        j = k - LAG
        if 0 <= j < PIECES:
            wait_bytes(piece(UP4, j), z_recv.at[j])
            pltpu.make_async_remote_copy(
                src_ref=piece(m_src, j), dst_ref=piece(UP1, j),
                send_sem=m_send, recv_sem=m_recv.at[j // 2], device_id=at(0, -1), device_id_type=MESH).start()
            if j < 24:
                pltpu.make_async_remote_copy(
                    src_ref=piece(p_src, j), dst_ref=piece(UP3, j),
                    send_sem=p_send, recv_sem=p_recv.at[j // 8], device_id=at(0, 1), device_id_type=MESH).start()

    def wait_m(quarter):
        for w in range(4):
            rows = blk.at[UP1, quarter, :, pl.ds(w * 256, 256), :]
            wait_bytes(rows, m_recv.at[quarter * 4 + w])

    def wait_p(quarter):
        wait_bytes(blk.at[UP3, quarter], p_recv.at[quarter])

    def turn(left, block, quarter):
        for ri in range(2):
            lt[left, ri, quarter * Q:(quarter + 1) * Q, :] = blk[block, quarter, ri].T

    def columns(block, quarters, ri):
        parts = [blk[block, q, ri] for q in quarters]
        return parts[0] if len(parts) == 1 else jnp.concatenate(parts, axis=1)

    def products(left, rows, re, im):
        lre, lim = lt[left, 0, rows, :], lt[left, 1, rows, :]
        dot = functools.partial(jnp.dot, preferred_element_type=F32)
        real = dot(lre, re) + dot(lim, im)
        imag = dot(lim, re) - dot(lre, im)
        return real, imag

    def factor(slot):
        return active[0, slot].astype(F32) * (1.0 / math.sqrt(K))

    def put_out(slot, rows, cols):
        pltpu.make_async_copy(ost.at[slot, :, rows, cols], out.at[slot, :, rows, cols], out_sem).start()

    def summary(slot, block, quarters):
        cols = pl.ds(quarters[0] * Q, len(quarters) * Q)
        scale = factor(slot)

        @pl.loop(0, 2)
        def _(half):
            rows = pl.ds(pl.multiple_of(half * 256, 256), 256)
            if block is None:
                re, im = a2[0], a2[1]
            else:
                re, im = columns(block, quarters, 0), columns(block, quarters, 1)
            real, imag = products(0, rows, re, im)
            ost[slot, 0, rows, cols] = (real * scale).astype(BF16)
            ost[slot, 1, rows, cols] = (imag * scale).astype(BF16)
            put_out(slot, rows, cols)

    def ret_copy(n, rows, cols):
        return pltpu.make_async_remote_copy(
            src_ref=rp.at[:, rows, cols], dst_ref=rv.at[:, rows, cols],
            send_sem=ret_send.at[n], recv_sem=ret_recv.at[n], device_id=nxt, device_id_type=MESH)

    def give_back(block, row_quarters, quarters):
        cols = pl.ds(quarters[0] * Q, len(quarters) * Q)
        rows = pl.ds(row_quarters[0] * Q, len(row_quarters) * Q)
        re, im = columns(block, quarters, 0), columns(block, quarters, 1)
        real, imag = products(1, rows, re, im)
        scale = 1.0 / math.sqrt(K)
        rp[0, rows, cols] = (real * scale).astype(BF16)
        rp[1, rows, cols] = (imag * scale).astype(BF16)

    def take_back(rows, cols, slot):
        flag = active[0, slot].astype(F32)
        ost[slot, :, rows, cols] = (rv[:, rows, cols].astype(F32) * flag).astype(BF16)
        put_out(slot, rows, cols)

    RETURNS = [
        (pl.ds(0, 256), pl.ds(0, 256)),
        (pl.ds(0, 256), pl.ds(256, 128)),
        (pl.ds(256, 128), pl.ds(0, 384)),
        (pl.ds(0, 384), pl.ds(384, 128)),
        (pl.ds(384, 128), pl.ds(0, 512)),
    ]

    def returned(n):
        ret_copy(n, *RETURNS[n]).start()

    def quantum(k):
        if k < 4:
            transform(k + 4)
        elif k == 10:
            turn(0, OWN, 0)
            turn(0, OWN, 1)
        elif k == 22:
            wait_m(0)
            wait_m(1)
            turn(1, UP1, 0)
            turn(1, UP1, 1)
        elif k == 23:
            wait_p(0)
            wait_p(1)
            give_back(UP3, (0, 1), (0, 1))
            returned(0)
        elif k == 24:
            turn(0, OWN, 2)
            turn(0, OWN, 3)
        elif k == 25:
            summary(0, OWN, (0, 1))
        elif k == 26:
            summary(0, OWN, (2, 3))
        elif k == 27:
            summary(4, UP4, (0, 1))
        elif k == 28:
            summary(1, UP1, (0, 1))
        elif k == 29:
            summary(3, UP3, (0, 1))
        elif k == 30:
            wait_p(2)
            give_back(UP3, (0, 1), (2,))
            returned(1)
        elif k == 31:
            wait_m(2)
            turn(1, UP1, 2)
            give_back(UP3, (2,), (0, 1))
            give_back(UP3, (2,), (2,))
            returned(2)
        elif k == 33:
            summary(3, UP3, (2,))

    @pl.loop(0, 4)
    def _(sc):
        transform(sc)

    for k in range(PIECES + LAG):
        tick(k)
        quantum(k)

    give_back(UP4, (0, 1, 2), (3,))
    returned(3)
    for w in range(4):
        rows = pl.ds(w * 256, 256)
        wait_bytes(blk.at[UP1, 3, :, rows, :], m_recv.at[12 + w])
        pltpu.make_async_remote_copy(
            src_ref=blk.at[UP1, 3, :, rows, :], dst_ref=a2.at[:, rows, :],
            send_sem=a2_send, recv_sem=a2_recv, device_id=prv, device_id_type=MESH).start()
    turn(1, UP1, 3)
    give_back(UP3, (3,), (0, 1))
    give_back(UP3, (3,), (2,))
    give_back(UP4, (3,), (3,))
    returned(4)
    summary(1, UP1, (2, 3))
    summary(4, UP4, (2, 3))

    for n in range(4):
        rows, cols = RETURNS[n]
        ret_copy(n, rows, cols).wait_recv()
        take_back(rows, cols, 3 if n == 3 else 2)
    wait_bytes(a2, a2_recv)
    summary(2, None, (3,))
    ret_copy(4, *RETURNS[4]).wait_recv()
    take_back(pl.ds(384, 128), pl.ds(0, 384), 2)
    take_back(pl.ds(384, 128), pl.ds(384, 128), 3)

    for n in range(5):
        ret_copy(n, *RETURNS[n]).wait_send()
    wait_bytes(a2, a2_send)
    wait_bytes(blk.at[OWN], z_send)
    wait_bytes(blk.at[OWN], m_send)
    wait_bytes(blk.at[OWN, pl.ds(0, 3)], p_send)
    for sc in range(8):
        wait_bytes(wh.at[sc, pl.ds(0, WIN - 1)], aa_send.at[sc])
    pltpu.make_async_copy(ost, out, out_sem).wait()


def shards(records, active):
    dma = pltpu.SemaphoreType.DMA
    out = pl.pallas_call(
        kernel,
        out_shape=jax.ShapeDtypeStruct((SLOTS, 2, ST, ST), BF16),
        in_specs=[
            pl.BlockSpec(memory_space=pltpu.SMEM),
            pl.BlockSpec(memory_space=pl.ANY),
            pl.BlockSpec(memory_space=pl.ANY),
        ],
        out_specs=pl.BlockSpec(memory_space=pl.ANY),
        scratch_shapes=[
            pltpu.VMEM((2 * BINS, SAMPLES), BF16),
            pltpu.VMEM((8, 2 * Q, SAMPLES), BF16),
            pltpu.VMEM((8, WIN, 2, 2, BAND_BINS, Q), BF16),
            pltpu.VMEM((4, 4, 2, K, Q), BF16),
            pltpu.VMEM((2, K, Q), BF16),
            pltpu.VMEM((2, 2, ST, K), BF16),
            pltpu.VMEM((2, ST, ST), BF16),
            pltpu.VMEM((2, ST, ST), BF16),
            pltpu.VMEM((SLOTS, 2, ST, ST), BF16),
            dma, dma((8,)), dma((8,)), dma((8,)), dma, dma((PIECES,)), dma, dma((16,)), dma, dma((3,)),
            dma, dma, dma((5,)), dma((5,)), dma,
        ],
        compiler_params=pltpu.CompilerParams(
            collective_id=0, has_side_effects=True, vmem_limit_bytes=60 * 2**20),
        cost_estimate=pl.CostEstimate(flops=20 * 2**30, bytes_accessed=25 * 2**20, transcendentals=0),
    )(active, records, jnp.asarray(spectral_table()))
    return out.reshape(1, SLOTS, 1, 2 * ST, ST)


def solution(mesh):
    return jax.shard_map(
        shards,
        mesh=mesh,
        in_specs=(P("win", "blk", None), P("blk", None)),
        out_specs=P("blk", None, "win", None, None),
        check_vma=False,
    )
```

time: 264 us -> 98.1 us (0.37)
  waiting for transfers between devices: 188 us -> 0 us
  Pallas kernels: 0 us -> 90.9 us
  matrix products: 24.8 us -> 0 us
  other arithmetic: 23.3 us -> 0 us
  starting transfers between devices: 13.7 us -> 0 us
  local copies, waits for them, and re-layouts: 10.6 us -> 5.41 us
  between operations: 3.26 us -> 0.01 us
    ppermute x4 -> x0, waiting for transfers between devices: 165 us -> none  [passed_along(): return lax.ppermute(x, axis, pairs)]
    pallas_call x0 -> x1, Pallas kernels: none -> 90.9 us  [shards(): pl.pallas_call(kernel, out_shape=jax.ShapeDtypeStruct((SLOTS, 2, ST, ST),...]
    dot_general x6 -> x0, matrix products: 24.8 us -> none  [the longest x1 12.5 us: shards(): jnp.einsum('wsn,nk->wsk', records, basis_table, preferred_element_type=jn...]
    all_to_all x1 -> x0, waiting for transfers between devices: 23.5 us -> none  [shards(): lax.all_to_all(by_bin, 'win', split_axis=1, concat_axis=0, tiled=True)]
    another operation x2 -> x0, other arithmetic: 19.1 us -> none
    ppermute x4 -> x0, starting transfers between devices: 9.15 us -> none  [passed_along(): return lax.ppermute(x, axis, pairs)]
    reshape x2 -> x0, local copies, waits for them, and re-layouts: 6.88 us -> none  [the longest x1 4.54 us: shards(): by_bin = by_bin.reshape(window_count, BINS, 2 * stations)]
    all_to_all x1 -> x0, starting transfers between devices: 4.6 us -> none  [shards(): lax.all_to_all(by_bin, 'win', split_axis=1, concat_axis=0, tiled=True)]
  transfers between devices with their start and end apart: 5 -> 0, of which waited for: 4 -> 0; matrix products, arithmetic and copies ran while one was open for 5% -> 0% of each run, Pallas kernels for 0% -> 0%
where the time goes in v1:
time: 98.1 us; the launch traced here: 96.4 us
  Pallas kernels  90.9 us (93%)
  local copies, waits for them, and re-layouts  5.41 us (6%)
    pallas_call x1, Pallas kernels, shards(): pl.pallas_call(kernel, out_shape=jax.ShapeDtypeStruct((SLOTS, 2, ST, ST),...  90.9 us
    unnamed x1, local copies, waits for them, and re-layouts  5.41 us

profile of v1, /device:TPU:6, one launch (start us, length us, event | category | flops | bytes accessed | tf_op | source)
XLA Modules:
  0.0 96.4 jit_solution(12538750732068553647)
XLA Ops:
  0.0 90.9 %shard_map.37 = bf16[5,2,512,512]{3,2,1,0:T(8,128)(2,1)} custom-call(s32[1,5]{1,0:T(1,128)} %active.1, bf16[4,512,4096]{2,1,0:T(8,128)(2,1)} %rec.1, bf16[512,4096]{1,0:T(8,128)(2,1)} %constant.2.clone.table), custom_call_target="tpu_custom_call" | custom-call | flops 21474836480 | bytes 26214400 | tf_op jit(solution)/shard_map/pallas_call | solution.py:292
  90.9 5.4 %copy.6 = bf16[1,5,1,1024,512]{4,3,2,1,0:T(8,128)(2,1)} copy(bf16[1,5,1,1024,512]{4,3,2,1,0:T(8,128)(2,1)} %bitcast.3) | data formatting | bytes 10485760

commit v2 on v0

v2 whole, which is shorter than its diff:
```python
import functools
import math

import jax
import jax.numpy as jnp
import ml_dtypes
import numpy as np
from jax import lax
from jax.experimental import pallas as pl
from jax.experimental.pallas import tpu as pltpu
from jax.sharding import PartitionSpec as P

SAMPLES = 4096
BINS = 256
BIN0 = 16
SLOTS = 5
BAND_BINS = 32
EPSILON = 1e-06

WIN = 8
RING = 4
BLOCKS = 16
LOCAL_W = 4
ST = 512
Q = 128
K = 1024
PIECES = 32
SLOTS_IN = 4

MESH = pl.DeviceIdType.MESH
F32 = jnp.float32
BF16 = jnp.bfloat16

OWN, UP4, UP1, UP3 = 0, 1, 2, 3


def spectral_table():
    phase = (np.arange(BINS)[:, None] + BIN0) * np.arange(SAMPLES)[None, :] % SAMPLES
    angles = phase.astype(np.float32) * np.float32(2.0 * math.pi / SAMPLES)
    angles = angles.astype(np.float64)
    return np.concatenate([np.cos(angles), -np.sin(angles)]).astype(np.float32).astype(ml_dtypes.bfloat16)


def pick(step, table, default=-1):
    value = jnp.int32(default)
    for at_step, entry in table.items():
        value = jnp.where(step == at_step, jnp.int32(entry), value)
    return value


START = 4
AHEAD = 3
TRANSFORM = {1: 1, 3: 2, 6: 3, 10: 4, 13: 5, 15: 6, 17: 7}
SPREAD = {2: 1, 5: 2, 6: 3, 10: 4, 13: 5, 15: 6, 17: 7}
GATHERED = {5: 1, 9: 2, 13: 3, 17: 4, 19: 5, 21: 6, 23: 7}
WAIT_M = {24: (0, 2), 30: (2, 3)}
WAIT_P = {25: (0, 2), 30: (2, 3)}
TURN = {13: (0, 0, 2), 23: (0, 2, 4), 24: (1, 0, 2), 30: (1, 2, 3), 37: (1, 3, 4)}
TILES = {25: (0, 2), 26: (2, 4), 30: (4, 6), 31: (6, 9), 35: (9, 12), 37: (12, 14), 38: (14, 16)}
RETURN = {28: (0,), 31: (1, 2), 35: (3,), 38: (4,)}
SUMMARY = {14: (0, 0, 0), 20: (4, 0, 0), 27: (1, 0, 0), 28: (3, 0, 0), 29: (0, 0, 1), 32: (0, 1, 0), 33: (0, 1, 1),
           34: (4, 1, 0), 36: (3, 1, 0), 39: (1, 1, 0), 40: (4, 0, 1), 41: (4, 1, 1), 42: (1, 0, 1), 43: (1, 1, 1)}
NARROW = {44: 2}
PART = {45: 0, 46: 1, 47: 2, 49: 3}
FORWARD = {35: (0, 2), 37: (2, 4)}
TAKE = {39: (0,), 45: (1, 2), 46: (3,), 48: (4,)}
STEPS = 50
TILE_AT = [(0, 0), (0, 1), (1, 0), (1, 1), (0, 2), (1, 2), (2, 0), (2, 1), (2, 2),
           (0, 3), (1, 3), (2, 3), (3, 0), (3, 1), (3, 2), (3, 3)]
TILES_OF = [(0, 4), (4, 6), (6, 9), (9, 12), (12, 16)]


def kernel(active_in, rec, table, out, active, tab, rbuf, wh, blk, lt, rp, rv, ost, acc,
           tab_sem, rec_sem, aa_send, aa_recv, z_send, z_recv, m_send, m_recv, p_send, p_recv,
           a2_send, a2_recv, ret_send, ret_recv, out_sem, active_sem):
    me = lax.axis_index("win")
    b = lax.axis_index("blk")
    z, x = b // RING, b % RING

    def peer(i):
        return (lax.rem(me + i, WIN), b)

    def at(dz, dx):
        return (me, lax.rem(z + dz + RING, RING) * RING + lax.rem(x + dx + RING, RING))

    nxt = (me, lax.rem(b + 1, BLOCKS))
    prv = (me, lax.rem(b + BLOCKS - 1, BLOCKS))

    def load(sc):
        slot = sc % SLOTS_IN
        return pltpu.make_async_copy(
            rec.at[sc % LOCAL_W, pl.ds(pl.multiple_of(sc // LOCAL_W * 2 * Q, 2 * Q), 2 * Q), :],
            rbuf.at[slot], rec_sem.at[slot])

    fetch = pltpu.make_async_copy(table, tab, tab_sem)
    fetch.start()
    load(0).start()
    flags = pltpu.make_async_copy(active_in, active, active_sem)
    flags.start()

    barrier = pltpu.get_barrier_semaphore()
    for i in range(1, WIN):
        pl.semaphore_signal(barrier, inc=1, device_id=peer(i), device_id_type=MESH)
    for dev in (at(-1, 0), at(1, 0), at(0, -1), at(0, 1), nxt, prv):
        pl.semaphore_signal(barrier, inc=1, device_id=dev, device_id_type=MESH)

    def transform(sc):
        load(sc).wait()
        spectra = lax.dot_general(
            tab[...], rbuf[sc % SLOTS_IN], (((1,), (1,)), ((), ())), preferred_element_type=F32)
        power = jnp.sum(spectra * spectra, axis=0, keepdims=True) / BINS
        white = (spectra * lax.rsqrt(power + EPSILON)).astype(BF16)
        for q in range(WIN):
            for ri in range(2):
                for qt in range(2):
                    wh[sc, q, qt, ri] = white[ri * BINS + q * BAND_BINS:ri * BINS + (q + 1) * BAND_BINS,
                                              qt * Q:(qt + 1) * Q]

        if isinstance(sc, int):
            load(sc + SLOTS_IN).start()
        else:
            @pl.when(sc + SLOTS_IN < 8)
            def _():
                load(sc + SLOTS_IN).start()

    def spread(sc, quarters, recv):
        h, w = sc // LOCAL_W, sc % LOCAL_W
        row = pl.multiple_of((w * WIN + me) * BAND_BINS, BAND_BINS)

        @pl.loop(1, WIN)
        def _(i):
            to = peer(i)
            pltpu.make_async_remote_copy(
                src_ref=wh.at[sc, to[0], quarters],
                dst_ref=blk.at[OWN, pl.ds(h * 2 + quarters.start, quarters.size), :, pl.ds(row, BAND_BINS), :],
                send_sem=aa_send.at[sc], recv_sem=aa_recv.at[recv], device_id=to, device_id_type=MESH,
            ).start()

        for qt in range(quarters.start, quarters.start + quarters.size):
            for ri in range(2):
                blk[OWN, h * 2 + qt, ri, pl.ds(row, BAND_BINS), :] = wh[sc, me, qt, ri]

    def place(j):
        early = j < 16
        return jnp.where(early, j // 2 % 2, j // 8), jnp.where(early, j // 4, j // 2 % 4)

    def piece(block, j):
        quarter, w = place(j)
        return blk.at[block, quarter, j % 2, pl.ds(pl.multiple_of(w * 256, 256), 256), :]

    def wait_bytes(ref, sem):
        pltpu.make_async_copy(ref, ref, sem).wait()

    def send_z(j):
        pltpu.make_async_remote_copy(
            src_ref=piece(OWN, j), dst_ref=piece(UP4, j),
            send_sem=z_send, recv_sem=z_recv.at[j], device_id=at(-1, 0), device_id_type=MESH).start()

    def send_m(block, j):
        quarter, w = place(j)
        pltpu.make_async_remote_copy(
            src_ref=piece(block, j), dst_ref=piece(UP1, j),
            send_sem=m_send, recv_sem=m_recv.at[quarter * 4 + w], device_id=at(0, -1), device_id_type=MESH).start()

    def send_p(block, j):
        quarter, _ = place(j)
        pltpu.make_async_remote_copy(
            src_ref=piece(block, j), dst_ref=piece(UP3, j),
            send_sem=p_send, recv_sem=p_recv.at[quarter], device_id=at(0, 1), device_id_type=MESH).start()

    def turn(left, quarter):
        block = jnp.where(left == 0, OWN, UP1)
        for ri in range(2):
            lt[left, ri, pl.ds(pl.multiple_of(quarter * Q, Q), Q), :] = blk[block, quarter, ri].T

    def products(left, rows, re, im, window=slice(None)):
        lre, lim = lt[left, 0, rows, window], lt[left, 1, rows, window]
        dot = functools.partial(jnp.dot, preferred_element_type=F32)
        real = dot(lre, re) + dot(lim, im)
        imag = dot(lim, re) - dot(lre, im)
        return real, imag

    def put_out(slot, rows, cols):
        pltpu.make_async_copy(ost.at[slot, :, rows, cols], out.at[slot, :, rows, cols], out_sem).start()

    def summary(slot, block, quarter, width, first, last):
        cols = pl.ds(pl.multiple_of(quarter * Q, Q), width * Q)
        scale = active[0, slot].astype(F32) * (1.0 / math.sqrt(K))

        @pl.loop(first, last)
        def _(half):
            rows = pl.ds(pl.multiple_of(half * 256, 256), 256)
            re = jnp.concatenate([blk[block, quarter + i, 0] for i in range(width)], axis=1)
            im = jnp.concatenate([blk[block, quarter + i, 1] for i in range(width)], axis=1)
            real, imag = products(0, rows, re, im)
            ost[slot, 0, rows, cols] = (real * scale).astype(BF16)
            ost[slot, 1, rows, cols] = (imag * scale).astype(BF16)
            put_out(slot, rows, cols)

    def part(w):
        window = pl.ds(pl.multiple_of(w * 256, 256), 256)
        wait_bytes(blk.at[UP3, 3, :, window, :], a2_recv.at[w])
        scale = active[0, 2].astype(F32) * (1.0 / math.sqrt(K))

        @pl.loop(0, 2)
        def _(half):
            rows = pl.ds(pl.multiple_of(half * 256, 256), 256)
            real, imag = products(0, rows, blk[UP3, 3, 0, window, :], blk[UP3, 3, 1, window, :], window)
            acc[0, rows, :] += real
            acc[1, rows, :] += imag

            @pl.when(w == 3)
            def _():
                cols = pl.ds(3 * Q, Q)
                ost[2, :, rows, cols] = (acc[:, rows, :] * scale).astype(BF16)
                put_out(2, rows, cols)

    def tile_at(n):
        return (pick(n, {i: rc[0] for i, rc in enumerate(TILE_AT)}, 0),
                pick(n, {i: rc[1] for i, rc in enumerate(TILE_AT)}, 0))

    def ret_copy(n):
        sl = [
            (pl.ds(0, 2), slice(None), pl.ds(0, 256)),
            (pl.ds(2, 1), slice(None), pl.ds(0, 256)),
            (pl.ds(0, 3), slice(None), pl.ds(256, 128)),
            (pl.ds(3, 1), slice(None), pl.ds(0, 384)),
            (pl.ds(0, 4), slice(None), pl.ds(384, 128)),
        ][n]
        return pltpu.make_async_remote_copy(
            src_ref=rp.at[sl], dst_ref=rv.at[sl],
            send_sem=ret_send.at[n], recv_sem=ret_recv.at[n], device_id=nxt, device_id_type=MESH)

    def give_back(n):
        r, c = tile_at(n)
        rows = pl.ds(pl.multiple_of(r * Q, Q), Q)
        block = jnp.where(c == 3, UP4, UP3)
        real, imag = products(1, rows, blk[block, c, 0], blk[block, c, 1])
        scale = 1.0 / math.sqrt(K)
        rp[c, 0, rows, :] = (real * scale).astype(BF16)
        rp[c, 1, rows, :] = (imag * scale).astype(BF16)

    def take_back(n):
        r, c = tile_at(n)
        rows, cols = pl.ds(pl.multiple_of(r * Q, Q), Q), pl.ds(pl.multiple_of(c * Q, Q), Q)
        slot = jnp.where(c == 3, 3, 2)
        flag = active[0, slot].astype(F32)
        ost[slot, :, rows, cols] = (rv[c, :, rows, :].astype(F32) * flag).astype(BF16)
        put_out(slot, rows, cols)

    def when_in(step, table):
        def run(body):
            entries = {k: v if isinstance(v, tuple) else (v,) for k, v in table.items()}
            first = pick(step, {k: v[0] for k, v in entries.items()})

            @pl.when(first >= 0)
            def _():
                rest = [pick(step, {k: v[i] for k, v in entries.items()}, 0)
                        for i in range(1, len(next(iter(entries.values()))))]
                body(first, *rest)
        return run

    fetch.wait()
    flags.wait()
    for sc in range(1, SLOTS_IN):
        load(sc).start()
    transform(0)
    pl.semaphore_wait(barrier, WIN - 1 + 6)
    spread(0, pl.ds(0, 1), 0)
    spread(0, pl.ds(1, 1), 8)
    acc[...] = jnp.zeros_like(acc)

    @pl.loop(1, STEPS)
    def _(step):
        k = step - START

        @pl.when((k >= 0) & (k < PIECES))
        def _():
            wait_bytes(piece(UP4, k), z_recv.at[k])

            @pl.when((x <= 2) & (k < 24))
            def _():
                send_p(UP4, k)

            @pl.when(x == 0)
            def _():
                send_m(UP4, k)

        @when_in(step, {START - 2: 0, START - 1: 8})
        def _(recv):
            wait_bytes(wh.at[0, pl.ds(0, WIN - 1), 0], aa_recv.at[recv])

        @when_in(step, GATHERED)
        def _(sc):
            wait_bytes(wh.at[sc, pl.ds(0, WIN - 1)], aa_recv.at[sc])

        lo = jnp.where(k < 0, 2 * (k + 2), k + AHEAD)
        hi = jnp.where(k < 0, jnp.maximum(lo, 0) + jnp.where(k >= -2, 2, 0), jnp.where(k >= 1, jnp.minimum(k + 1 + AHEAD, PIECES), 0))
        lo = jnp.maximum(lo, 0)

        @pl.loop(lo, hi)
        def _(j):
            send_z(j)

            @pl.when(x >= 1)
            def _():
                send_m(OWN, j)

            @pl.when((x == 3) & (j < 24))
            def _():
                send_p(OWN, j)

        @when_in(step, FORWARD)
        def _(first, last):
            @pl.loop(first, last)
            def _(w):
                rows = pl.ds(pl.multiple_of(w * 256, 256), 256)
                wait_bytes(blk.at[UP1, 3, :, rows, :], m_recv.at[12 + w])
                pltpu.make_async_remote_copy(
                    src_ref=blk.at[UP1, 3, :, rows, :], dst_ref=blk.at[UP3, 3, :, rows, :],
                    send_sem=a2_send, recv_sem=a2_recv.at[w], device_id=prv, device_id_type=MESH).start()

        @when_in(step, TRANSFORM)
        def _(sc):
            transform(sc)

        @when_in(step, SPREAD)
        def _(sc):
            spread(sc, pl.ds(0, 2), sc)

        @when_in(step, WAIT_M)
        def _(first, last):
            @pl.loop(first * 4, last * 4)
            def _(i):
                rows = pl.ds(pl.multiple_of(i % 4 * 256, 256), 256)
                wait_bytes(blk.at[UP1, i // 4, :, rows, :], m_recv.at[i])

        @when_in(step, WAIT_P)
        def _(first, last):
            @pl.loop(first, last)
            def _(quarter):
                wait_bytes(blk.at[UP3, quarter], p_recv.at[quarter])

        @when_in(step, TURN)
        def _(left, first, last):
            @pl.loop(first, last)
            def _(quarter):
                turn(left, quarter)

        @when_in(step, TILES)
        def _(first, last):
            @pl.loop(first, last)
            def _(n):
                give_back(n)

        for at_step, ns in RETURN.items():
            @pl.when(step == at_step)
            def _():
                for n in ns:
                    ret_copy(n).start()

        @when_in(step, SUMMARY)
        def _(slot, half, pair):
            block = pick(slot, {0: OWN, 1: UP1, 3: UP3, 4: UP4}, 0)
            summary(slot, block, pair * 2, 2, half, half + 1)

        @when_in(step, NARROW)
        def _(quarter):
            summary(3, UP3, quarter, 1, 0, 2)

        @when_in(step, PART)
        def _(w):
            part(w)

        for at_step, ns in TAKE.items():
            @pl.when(step == at_step)
            def _():
                for n in ns:
                    ret_copy(n).wait_recv()

        tiles = {k: (TILES_OF[ns[0]][0], TILES_OF[ns[-1]][1]) for k, ns in TAKE.items()}

        @when_in(step, tiles)
        def _(first, last):
            @pl.loop(first, last)
            def _(n):
                take_back(n)

    for n in range(5):
        ret_copy(n).wait_send()
    wait_bytes(blk.at[UP3, 3], a2_send)
    wait_bytes(blk.at[OWN], z_send)
    wait_bytes(blk.at[OWN], m_send)
    wait_bytes(blk.at[OWN, pl.ds(0, 3)], p_send)
    for sc in range(8):
        wait_bytes(wh.at[sc, pl.ds(0, WIN - 1)], aa_send.at[sc])
    pltpu.make_async_copy(ost, out, out_sem).wait()


def shards(records, active):
    dma = pltpu.SemaphoreType.DMA
    out = pl.pallas_call(
        kernel,
        out_shape=jax.ShapeDtypeStruct((SLOTS, 2, ST, ST), BF16),
        in_specs=[
            pl.BlockSpec(memory_space=pltpu.HBM),
            pl.BlockSpec(memory_space=pltpu.HBM),
            pl.BlockSpec(memory_space=pltpu.HBM),
        ],
        out_specs=pl.BlockSpec(memory_space=pl.ANY),
        scratch_shapes=[
            pltpu.SMEM((1, SLOTS), jnp.int32),
            pltpu.VMEM((2 * BINS, SAMPLES), BF16),
            pltpu.VMEM((SLOTS_IN, 2 * Q, SAMPLES), BF16),
            pltpu.VMEM((8, WIN, 2, 2, BAND_BINS, Q), BF16),
            pltpu.VMEM((4, 4, 2, K, Q), BF16),
            pltpu.VMEM((2, 2, ST, K), BF16),
            pltpu.VMEM((4, 2, ST, Q), BF16),
            pltpu.VMEM((4, 2, ST, Q), BF16),
            pltpu.VMEM((SLOTS, 2, ST, ST), BF16),
            pltpu.VMEM((2, ST, Q), F32),
            dma, dma((SLOTS_IN,)), dma((8,)), dma((9,)), dma, dma((PIECES,)), dma, dma((16,)), dma, dma((3,)),
            dma, dma((4,)), dma((5,)), dma((5,)), dma, dma,
        ],
        compiler_params=pltpu.CompilerParams(
            collective_id=0, has_side_effects=True, vmem_limit_bytes=42 * 2**20),
        cost_estimate=pl.CostEstimate(flops=20 * 2**30, bytes_accessed=25 * 2**20, transcendentals=0),
    )(pltpu.with_memory_space_constraint(active, pltpu.HBM), records, pltpu.with_memory_space_constraint(jnp.asarray(spectral_table()), pltpu.HBM))
    return out.reshape(1, SLOTS, 1, 2 * ST, ST)


def solution(mesh):
    return jax.shard_map(
        shards,
        mesh=mesh,
        in_specs=(P("win", "blk", None), P("blk", None)),
        out_specs=P("blk", None, "win", None, None),
        check_vma=False,
    )
```

time: 264 us -> 79.9 us (0.30)
  waiting for transfers between devices: 188 us -> 0 us
  Pallas kernels: 0 us -> 77.4 us
  matrix products: 24.8 us -> 0 us
  other arithmetic: 23.3 us -> 0 us
  starting transfers between devices: 13.7 us -> 0 us
  local copies, waits for them, and re-layouts: 10.6 us -> 2.36 us
  between operations: 3.26 us -> 0.01 us
    ppermute x4 -> x0, waiting for transfers between devices: 165 us -> none  [passed_along(): return lax.ppermute(x, axis, pairs)]
    pallas_call x0 -> x1, Pallas kernels: none -> 77.4 us  [shards(): pl.pallas_call(kernel, out_shape=jax.ShapeDtypeStruct((SLOTS, 2, ST, ST),...]
    dot_general x6 -> x0, matrix products: 24.8 us -> none  [the longest x1 12.5 us: shards(): jnp.einsum('wsn,nk->wsk', records, basis_table, preferred_element_type=jn...]
    all_to_all x1 -> x0, waiting for transfers between devices: 23.5 us -> none  [shards(): lax.all_to_all(by_bin, 'win', split_axis=1, concat_axis=0, tiled=True)]
    another operation x2 -> x0, other arithmetic: 19.1 us -> none
    ppermute x4 -> x0, starting transfers between devices: 9.15 us -> none  [passed_along(): return lax.ppermute(x, axis, pairs)]
    reshape x2 -> x0, local copies, waits for them, and re-layouts: 6.88 us -> none  [the longest x1 4.54 us: shards(): by_bin = by_bin.reshape(window_count, BINS, 2 * stations)]
    all_to_all x1 -> x0, starting transfers between devices: 4.6 us -> none  [shards(): lax.all_to_all(by_bin, 'win', split_axis=1, concat_axis=0, tiled=True)]
  transfers between devices with their start and end apart: 5 -> 0, of which waited for: 4 -> 0; matrix products, arithmetic and copies ran while one was open for 5% -> 0% of each run, Pallas kernels for 0% -> 0%
where the time goes in v2:
time: 79.9 us; the launch traced here: 79.8 us
  Pallas kernels  77.4 us (97%)
  local copies, waits for them, and re-layouts  2.36 us (3%)
    pallas_call x1, Pallas kernels, shards(): pl.pallas_call(kernel, out_shape=jax.ShapeDtypeStruct((SLOTS, 2, ST, ST),...  77.4 us
    unnamed x1, local copies, waits for them, and re-layouts  2.36 us

profile of v2, /device:TPU:6, one launch (start us, length us, event | category | flops | bytes accessed | tf_op | source)
XLA Modules:
  0.0 79.8 jit_solution(2173052361021754280)
XLA Ops:
  0.0 77.4 %shard_map.37 = bf16[5,2,512,512]{3,2,1,0:T(8,128)(2,1)S(1)} custom-call(s32[1,5]{1,0:T(1,128)} %active_in.1, bf16[4,512,4096]{2,1,0:T(8,128)(2,1)} %rec.1, bf16[512,4096]{1,0:T(8,128)(2,1)} %constant.2.clone.table), custom_call_target="tpu_custom_call" | custom-call | flops 21474836480 | bytes 26214400 | tf_op jit(solution)/shard_map/pallas_call | solution.py:402
  77.4 2.4 %copy.6 = bf16[1,5,1,1024,512]{4,3,2,1,0:T(8,128)(2,1)} copy(bf16[1,5,1,1024,512]{4,3,2,1,0:T(8,128)(2,1)S(1)} %bitcast.3) | data formatting | bytes 10485760

commit v3 on v2

v3 whole, which is shorter than its diff:
```python
import functools
import math

import jax
import jax.numpy as jnp
import ml_dtypes
import numpy as np
from jax import lax
from jax.experimental import pallas as pl
from jax.experimental.pallas import tpu as pltpu
from jax.sharding import PartitionSpec as P

SAMPLES = 4096
BINS = 256
BIN0 = 16
SLOTS = 5
BAND_BINS = 32
EPSILON = 1e-06

WIN = 8
RING = 4
BLOCKS = 16
LOCAL_W = 4
ST = 512
Q = 128
K = 1024
PIECES = 32
SLOTS_IN = 4

MESH = pl.DeviceIdType.MESH
F32 = jnp.float32
BF16 = jnp.bfloat16

OWN, UP4, UP1, UP3 = 0, 1, 2, 3


def spectral_table():
    phase = (np.arange(BINS)[:, None] + BIN0) * np.arange(HALF)[None, :] % SAMPLES
    angles = phase.astype(np.float32) * np.float32(2.0 * math.pi / SAMPLES)
    angles = angles.astype(np.float64)
    return np.concatenate([np.cos(angles), -np.sin(angles)]).astype(np.float32).astype(ml_dtypes.bfloat16)


def pick(k, table, default=-1):
    value = jnp.int32(default)
    for at_k, entry in table.items():
        value = jnp.where(k == at_k, jnp.int32(entry), value)
    return value


FIRST_STEP, LAST_STEP = -5, 43
HALF = SAMPLES // 2
PART_COLS = HALF // 4
AHEAD = 3
MORE_AHEAD = 8
FIRST = 8
TRANSFORM = {-5: 1, -1: 2, 2: 3, 6: 4, 9: 5, 11: 6, 13: 7}
SPREAD = {-4: 1, 1: 2, 2: 3, 6: 4, 9: 5, 11: 6, 13: 7}
GATHERED = {1: 1, 5: 2, 8: 3, 12: 4, 14: 5, 16: 6, 18: 7}
WAIT_M = {20: (0, 2), 26: (2, 3)}
WAIT_P = {21: (0, 2), 26: (2, 3)}
TURN = {9: (0, 0, 2), 19: (0, 2, 4), 20: (1, 0, 2), 26: (1, 2, 3), 33: (1, 3, 4)}
BACK_HALF = {21: 0}
BACK_TALL = {27: 2, 31: 3}
BACK_WIDE = {26: (2, 0), 33: (3, 0), 34: (3, 1)}
RETURN = {24: (0,), 27: (1, 2), 31: (3,), 34: (4,)}
RETURN_EARLY = 21
SUMMARY = {10: (0, 0, 0), 16: (4, 0, 0), 22: (1, 0, 0), 23: (3, 0, 0), 24: (0, 0, 1), 25: (0, 1, 0), 28: (0, 1, 1),
           29: (4, 1, 0), 30: (3, 1, 0), 32: (1, 1, 0), 35: (4, 0, 1), 36: (4, 1, 1), 37: (1, 0, 1), 38: (1, 1, 1)}
PART = {39: 0, 40: 1, 41: 2, 42: 3}
FORWARD = {33: (0, 4)}
TAKE = {31: (0,), 39: (1, 2), 41: (3,), 43: (4,)}
TILE_AT = [(0, 0), (0, 1), (1, 0), (1, 1), (0, 2), (1, 2), (2, 2), (2, 0), (2, 1),
           (0, 3), (1, 3), (2, 3), (3, 0), (3, 1), (3, 2), (3, 3)]
TILES_OF = [(0, 4), (4, 7), (7, 9), (9, 12), (12, 16)]


def kernel(active_in, rec, table, out, active, tab, rbuf, wh, blk, lt, rp, rv, ost, acc,
           tab_sem, first_sem, later_sem, rec_sem, aa_send, aa_recv, z_send, z_recv, m_send, m_recv, p_send, p_recv,
           a2_send, a2_recv, ret_send, ret_recv, out_sem, active_sem):
    me = lax.axis_index("win")
    b = lax.axis_index("blk")
    z, x = b // RING, b % RING

    def peer(i):
        return (lax.rem(me + i, WIN), b)

    def at(dz, dx):
        return (me, lax.rem(z + dz + RING, RING) * RING + lax.rem(x + dx + RING, RING))

    nxt = (me, lax.rem(b + 1, BLOCKS))
    prv = (me, lax.rem(b + BLOCKS - 1, BLOCKS))

    def load(sc):
        slot = sc % SLOTS_IN
        return pltpu.make_async_copy(
            rec.at[sc % LOCAL_W, pl.ds(pl.multiple_of(sc // LOCAL_W * 2 * Q, 2 * Q), 2 * Q), :],
            rbuf.at[slot], rec_sem.at[slot])

    def fetch(part):
        cols = pl.ds(pl.multiple_of(part * PART_COLS, PART_COLS), PART_COLS)
        later = pl.ds(pl.multiple_of(HALF + part * PART_COLS, PART_COLS), PART_COLS)
        return (pltpu.make_async_copy(table.at[:, cols], tab.at[:, cols], tab_sem.at[part]),
                pltpu.make_async_copy(rec.at[0, pl.ds(0, 2 * Q), cols], rbuf.at[0, :, cols], first_sem.at[part]),
                pltpu.make_async_copy(rec.at[0, pl.ds(0, 2 * Q), later], rbuf.at[0, :, later], later_sem.at[part]))

    for part in range(4):
        for copy in fetch(part):
            copy.start()
    flags = pltpu.make_async_copy(active_in, active, active_sem)
    flags.start()

    barrier = pltpu.get_barrier_semaphore()
    for i in range(1, WIN):
        pl.semaphore_signal(barrier, inc=1, device_id=peer(i), device_id_type=MESH)
    for dev in (at(-1, 0), at(1, 0), at(0, -1), at(0, 1), nxt, prv):
        pl.semaphore_signal(barrier, inc=1, device_id=dev, device_id_type=MESH)

    def against(table_rows, rows):
        return lax.dot_general(table_rows, rows, (((1,), (1,)), ((), ())), preferred_element_type=F32)

    def transform(sc):
        load(sc).wait()
        slot = sc % SLOTS_IN
        whiten(sc, against(tab[...], rbuf[slot, :, pl.ds(0, HALF)]), against(tab[...], rbuf[slot, :, pl.ds(HALF, HALF)]))

    def first_transform():
        acc[...] = jnp.zeros_like(acc)

        @pl.loop(0, 4)
        def _(part):
            for copy in fetch(part):
                copy.wait()
            cols = pl.ds(pl.multiple_of(part * PART_COLS, PART_COLS), PART_COLS)
            later = pl.ds(pl.multiple_of(HALF + part * PART_COLS, PART_COLS), PART_COLS)
            acc[0] += against(tab[:, cols], rbuf[0, :, cols])
            acc[1] += against(tab[:, cols], rbuf[0, :, later])

        for sc in range(1, SLOTS_IN):
            load(sc).start()
        whiten(0, acc[0], acc[1])

    def whiten(sc, early, later):
        odd = lax.broadcasted_iota(jnp.int32, early.shape, 0) % 2 == 1
        spectra = early + jnp.where(odd, -later, later)
        power = jnp.sum(spectra * spectra, axis=0, keepdims=True) / BINS
        white = (spectra * lax.rsqrt(power + EPSILON)).astype(BF16)
        for q in range(WIN):
            for ri in range(2):
                for qt in range(2):
                    wh[sc, q, qt, ri] = white[ri * BINS + q * BAND_BINS:ri * BINS + (q + 1) * BAND_BINS,
                                              qt * Q:(qt + 1) * Q]

        if isinstance(sc, int):
            load(sc + SLOTS_IN).start()
        else:
            @pl.when(sc + SLOTS_IN < 8)
            def _():
                load(sc + SLOTS_IN).start()

    def spread(sc, part=None):
        h, w = sc // LOCAL_W, sc % LOCAL_W
        row = pl.multiple_of((w * WIN + me) * BAND_BINS, BAND_BINS)

        @pl.loop(1, WIN)
        def _(i):
            to = peer(i)
            if part is None:
                src = wh.at[sc, to[0]]
                dst = blk.at[OWN, pl.ds(h * 2, 2), :, pl.ds(row, BAND_BINS), :]
            else:
                src = wh.at[sc, to[0], part // 2, part % 2]
                dst = blk.at[OWN, part // 2, part % 2, pl.ds(row, BAND_BINS), :]
            pltpu.make_async_remote_copy(
                src_ref=src, dst_ref=dst, send_sem=aa_send.at[sc],
                recv_sem=aa_recv.at[sc if part is None else FIRST + part],
                device_id=to, device_id_type=MESH,
            ).start()

        for own in range(4) if part is None else (part,):
            blk[OWN, h * 2 + own // 2, own % 2, pl.ds(row, BAND_BINS), :] = wh[sc, me, own // 2, own % 2]

    def place(j):
        early = j < 16
        return jnp.where(early, j // 2 % 2, j // 8), jnp.where(early, j // 4, j // 2 % 4)

    def piece(block, j):
        quarter, w = place(j)
        return blk.at[block, quarter, j % 2, pl.ds(pl.multiple_of(w * 256, 256), 256), :]

    def wait_bytes(ref, sem):
        pltpu.make_async_copy(ref, ref, sem).wait()

    def send_z(j):
        pltpu.make_async_remote_copy(
            src_ref=piece(OWN, j), dst_ref=piece(UP4, j),
            send_sem=z_send, recv_sem=z_recv.at[j], device_id=at(-1, 0), device_id_type=MESH).start()

    def send_m(block, j):
        quarter, w = place(j)
        pltpu.make_async_remote_copy(
            src_ref=piece(block, j), dst_ref=piece(UP1, j),
            send_sem=m_send, recv_sem=m_recv.at[quarter * 4 + w], device_id=at(0, -1), device_id_type=MESH).start()

    def send_p(block, j):
        quarter, _ = place(j)
        pltpu.make_async_remote_copy(
            src_ref=piece(block, j), dst_ref=piece(UP3, j),
            send_sem=p_send, recv_sem=p_recv.at[quarter], device_id=at(0, 1), device_id_type=MESH).start()

    def turn(left, quarter):
        block = jnp.where(left == 0, OWN, UP1)
        for ri in range(2):
            lt[left, ri, pl.ds(pl.multiple_of(quarter * Q, Q), Q), :] = blk[block, quarter, ri].T

    def products(left, rows, re, im, window=slice(None)):
        lre, lim = lt[left, 0, rows, window], lt[left, 1, rows, window]
        dot = functools.partial(jnp.dot, preferred_element_type=F32)
        real = dot(lre, re) + dot(lim, im)
        imag = dot(lim, re) - dot(lre, im)
        return real, imag

    def put_out(slot, rows, cols):
        pltpu.make_async_copy(ost.at[slot, :, rows, cols], out.at[slot, :, rows, cols], out_sem).start()

    def summary(slot, block, half, pair):
        rows = pl.ds(pl.multiple_of(half * 256, 256), 256)
        cols = pl.ds(pl.multiple_of(pair * 256, 256), 256)
        scale = active[0, slot].astype(F32) * (1.0 / math.sqrt(K))
        re, im = [jnp.concatenate([blk[block, pair * 2 + i, ri] for i in range(2)], axis=1) for ri in range(2)]
        real, imag = products(0, rows, re, im)
        ost[slot, 0, rows, cols] = (real * scale).astype(BF16)
        ost[slot, 1, rows, cols] = (imag * scale).astype(BF16)
        put_out(slot, rows, cols)

    def add_windows(w):
        window = pl.ds(pl.multiple_of(w * 256, 256), 256)
        wait_bytes(blk.at[UP3, 3, :, window, :], a2_recv.at[w])

        @pl.loop(0, 2)
        def _(half):
            rows = pl.ds(pl.multiple_of(half * 256, 256), 256)
            re, im = [jnp.concatenate([blk[UP3, c, ri, window, :] for c in (2, 3)], axis=1) for ri in range(2)]
            real, imag = products(0, rows, re, im, window)
            acc[0, rows, :] += real
            acc[1, rows, :] += imag

            @pl.when(w == 3)
            def _():
                for slot, c in ((3, 2), (2, 3)):
                    scale = active[0, slot].astype(F32) * (1.0 / math.sqrt(K))
                    cols = pl.ds(c * Q, Q)
                    ost[slot, :, rows, cols] = (acc[:, rows, (c - 2) * Q:(c - 1) * Q] * scale).astype(BF16)
                    put_out(slot, rows, cols)

    def tile_at(n):
        return (pick(n, {i: rc[0] for i, rc in enumerate(TILE_AT)}, 0),
                pick(n, {i: rc[1] for i, rc in enumerate(TILE_AT)}, 0))

    def ret_copy(n):
        sl = [
            (pl.ds(0, 2), slice(None), pl.ds(0, 256)),
            (pl.ds(2, 1), slice(None), pl.ds(0, 384)),
            (pl.ds(0, 2), slice(None), pl.ds(256, 128)),
            (pl.ds(3, 1), slice(None), pl.ds(0, 384)),
            (pl.ds(0, 4), slice(None), pl.ds(384, 128)),
        ][n]
        return pltpu.make_async_remote_copy(
            src_ref=rp.at[sl], dst_ref=rv.at[sl],
            send_sem=ret_send.at[n], recv_sem=ret_recv.at[n], device_id=nxt, device_id_type=MESH)

    def give_back(rows, quarters):
        parts = [[blk[jnp.where(c == 3, UP4, UP3), c, ri] for c in quarters] for ri in range(2)]
        re, im = [p[0] if len(p) == 1 else jnp.concatenate(p, axis=1) for p in parts]
        scale = 1.0 / math.sqrt(K)
        for ri, product in enumerate(products(1, rows, re, im)):
            scaled = (product * scale).astype(BF16)
            for i, c in enumerate(quarters):
                rp[c, ri, rows, :] = scaled[:, i * Q:(i + 1) * Q]

    def take_back(n):
        r, c = tile_at(n)
        rows, cols = pl.ds(pl.multiple_of(r * Q, Q), Q), pl.ds(pl.multiple_of(c * Q, Q), Q)
        slot = jnp.where(c == 3, 3, 2)
        flag = active[0, slot].astype(F32)
        ost[slot, :, rows, cols] = (rv[c, :, rows, :].astype(F32) * flag).astype(BF16)
        put_out(slot, rows, cols)

    def when_in(k, table):
        def run(body):
            entries = {key: v if isinstance(v, tuple) else (v,) for key, v in table.items()}
            first = pick(k, {key: v[0] for key, v in entries.items()})

            @pl.when(first >= 0)
            def _():
                rest = [pick(k, {key: v[i] for key, v in entries.items()}, 0)
                        for i in range(1, len(next(iter(entries.values()))))]
                body(first, *rest)
        return run

    flags.wait()
    first_transform()
    pl.semaphore_wait(barrier, WIN - 1 + 6)
    for part in range(4):
        spread(0, part)
    acc[...] = jnp.zeros_like(acc)

    @pl.loop(0, LAST_STEP - FIRST_STEP + 1)
    def _(step):
        k = step + FIRST_STEP

        @pl.when((k >= 0) & (k < PIECES))
        def _():
            wait_bytes(piece(UP4, k), z_recv.at[k])

            @pl.when((x <= 2) & (k < 24))
            def _():
                send_p(UP4, k)

            @pl.when(x == 0)
            def _():
                send_m(UP4, k)

        @pl.when((k >= -4) & (k < 0))
        def _():
            wait_bytes(wh.at[0, pl.ds(0, WIN - 1), 0, 0], aa_recv.at[FIRST + 4 + k])

        @when_in(k, GATHERED)
        def _(sc):
            wait_bytes(wh.at[sc, pl.ds(0, WIN - 1)], aa_recv.at[sc])

        lo = jnp.where(k < 0, k + 4, k + AHEAD + jnp.where(k > MORE_AHEAD, 1, 0))
        count = jnp.where((k >= -4) & (k != 0) & (lo < PIECES), jnp.where(k == MORE_AHEAD, 2, 1), 0)
        hi = lo + count

        @pl.loop(lo, hi)
        def _(j):
            send_z(j)

            @pl.when(x >= 1)
            def _():
                send_m(OWN, j)

            @pl.when((x == 3) & (j < 24))
            def _():
                send_p(OWN, j)

        @when_in(k, FORWARD)
        def _(first, last):
            @pl.loop(first, last)
            def _(w):
                rows = pl.ds(pl.multiple_of(w * 256, 256), 256)
                wait_bytes(blk.at[UP1, 3, :, rows, :], m_recv.at[12 + w])
                pltpu.make_async_remote_copy(
                    src_ref=blk.at[UP1, 3, :, rows, :], dst_ref=blk.at[UP3, 3, :, rows, :],
                    send_sem=a2_send, recv_sem=a2_recv.at[w], device_id=prv, device_id_type=MESH).start()

        @when_in(k, TRANSFORM)
        def _(sc):
            transform(sc)

        @when_in(k, SPREAD)
        def _(sc):
            spread(sc)

        @when_in(k, WAIT_M)
        def _(first, last):
            @pl.loop(first * 4, last * 4)
            def _(i):
                rows = pl.ds(pl.multiple_of(i % 4 * 256, 256), 256)
                wait_bytes(blk.at[UP1, i // 4, :, rows, :], m_recv.at[i])

        @when_in(k, WAIT_P)
        def _(first, last):
            @pl.loop(first, last)
            def _(quarter):
                wait_bytes(blk.at[UP3, quarter], p_recv.at[quarter])

        @when_in(k, TURN)
        def _(left, first, last):
            @pl.loop(first, last)
            def _(quarter):
                turn(left, quarter)

        @when_in(k, BACK_HALF)
        def _(_):
            give_back(pl.ds(0, 256), (0, 1))

        @when_in(k, BACK_TALL)
        def _(quarter):
            give_back(pl.ds(0, 384), (quarter,))

        @when_in(k, BACK_WIDE)
        def _(quarter, pair):
            give_back(pl.ds(pl.multiple_of(quarter * Q, Q), Q), (pair * 2, pair * 2 + 1))

        for at_k, ns in RETURN.items():
            now = k == (at_k if ns != (0,) else jnp.where(x == 3, RETURN_EARLY, at_k))

            @pl.when(now)
            def _():
                for n in ns:
                    ret_copy(n).start()

        @when_in(k, SUMMARY)
        def _(slot, half, pair):
            block = pick(slot, {0: OWN, 1: UP1, 3: UP3, 4: UP4}, 0)
            summary(slot, block, half, pair)

        @when_in(k, PART)
        def _(w):
            add_windows(w)

        for at_k, ns in TAKE.items():
            @pl.when(k == at_k)
            def _():
                for n in ns:
                    ret_copy(n).wait_recv()

        tiles = {key: (TILES_OF[ns[0]][0], TILES_OF[ns[-1]][1]) for key, ns in TAKE.items()}

        @when_in(k, tiles)
        def _(first, last):
            @pl.loop(first, last)
            def _(n):
                take_back(n)

    for n in range(5):
        ret_copy(n).wait_send()
    wait_bytes(blk.at[UP3, 3], a2_send)
    wait_bytes(blk.at[OWN], z_send)
    wait_bytes(blk.at[OWN], m_send)
    wait_bytes(blk.at[OWN, pl.ds(0, 3)], p_send)
    for sc in range(8):
        wait_bytes(wh.at[sc, pl.ds(0, WIN - 1)], aa_send.at[sc])
    pltpu.make_async_copy(ost, out, out_sem).wait()


def shards(records, active):
    dma = pltpu.SemaphoreType.DMA
    out = pl.pallas_call(
        kernel,
        out_shape=jax.ShapeDtypeStruct((SLOTS, 2, ST, ST), BF16),
        in_specs=[
            pl.BlockSpec(memory_space=pltpu.HBM),
            pl.BlockSpec(memory_space=pltpu.HBM),
            pl.BlockSpec(memory_space=pltpu.HBM),
        ],
        out_specs=pl.BlockSpec(memory_space=pl.ANY),
        scratch_shapes=[
            pltpu.SMEM((1, SLOTS), jnp.int32),
            pltpu.VMEM((2 * BINS, HALF), BF16),
            pltpu.VMEM((SLOTS_IN, 2 * Q, SAMPLES), BF16),
            pltpu.VMEM((8, WIN, 2, 2, BAND_BINS, Q), BF16),
            pltpu.VMEM((4, 4, 2, K, Q), BF16),
            pltpu.VMEM((2, 2, ST, K), BF16),
            pltpu.VMEM((4, 2, ST, Q), BF16),
            pltpu.VMEM((4, 2, ST, Q), BF16),
            pltpu.VMEM((SLOTS, 2, ST, ST), BF16),
            pltpu.VMEM((2, ST, 2 * Q), F32),
            dma((4,)), dma((4,)), dma((4,)), dma((SLOTS_IN,)), dma((8,)), dma((FIRST + 4,)), dma, dma((PIECES,)), dma, dma((16,)), dma, dma((3,)),
            dma, dma((4,)), dma((5,)), dma((5,)), dma, dma,
        ],
        compiler_params=pltpu.CompilerParams(
            collective_id=0, has_side_effects=True, vmem_limit_bytes=42 * 2**20),
        cost_estimate=pl.CostEstimate(flops=20 * 2**30, bytes_accessed=25 * 2**20, transcendentals=0),
    )(pltpu.with_memory_space_constraint(active, pltpu.HBM), records, pltpu.with_memory_space_constraint(jnp.asarray(spectral_table()), pltpu.HBM))
    return out.reshape(1, SLOTS, 1, 2 * ST, ST)


def solution(mesh):
    return jax.shard_map(
        shards,
        mesh=mesh,
        in_specs=(P("win", "blk", None), P("blk", None)),
        out_specs=P("blk", None, "win", None, None),
        check_vma=False,
    )
```

time: 79.9 us -> 78.7 us (0.985)
  Pallas kernels: 77.4 us -> 75.8 us
    pallas_call x1, Pallas kernels: 77.4 us -> 75.8 us  [shards(): pl.pallas_call(kernel, out_shape=jax.ShapeDtypeStruct((SLOTS, 2, ST, ST),...]
where the time goes in v3:
time: 78.7 us; the launch traced here: 78.2 us
  Pallas kernels  75.8 us (96%)
  local copies, waits for them, and re-layouts  2.36 us (3%)
    pallas_call x1, Pallas kernels, shards(): pl.pallas_call(kernel, out_shape=jax.ShapeDtypeStruct((SLOTS, 2, ST, ST),...  75.8 us
    unnamed x1, local copies, waits for them, and re-layouts  2.36 us

profile of v3, /device:TPU:6, one launch (start us, length us, event | category | flops | bytes accessed | tf_op | source)
XLA Modules:
  0.0 78.2 jit_solution(976357090474500566)
XLA Ops:
  0.0 75.8 %shard_map.37 = bf16[5,2,512,512]{3,2,1,0:T(8,128)(2,1)S(1)} custom-call(s32[1,5]{1,0:T(1,128)} %active_in.1, bf16[4,512,4096]{2,1,0:T(8,128)(2,1)} %rec.1, bf16[512,2048]{1,0:T(8,128)(2,1)} %constant.2.clone.table), custom_call_target="tpu_custom_call" | custom-call | flops 21474836480 | bytes 26214400 | tf_op jit(solution)/shard_map/pallas_call | solution.py:441
  75.8 2.4 %copy.6 = bf16[1,5,1,1024,512]{4,3,2,1,0:T(8,128)(2,1)} copy(bf16[1,5,1,1024,512]{4,3,2,1,0:T(8,128)(2,1)S(1)} %bitcast.3) | data formatting | bytes 10485760

commit v4 on v3

--- a/solution.py
+++ b/solution.py
@@ -51,12 +51,12 @@
 FIRST_STEP, LAST_STEP = -5, 43
 HALF = SAMPLES // 2
 PART_COLS = HALF // 4
-AHEAD = 3
-MORE_AHEAD = 8
+SINGLE = 4
+AHEAD = 4
 FIRST = 8
 TRANSFORM = {-5: 1, -1: 2, 2: 3, 6: 4, 9: 5, 11: 6, 13: 7}
-SPREAD = {-4: 1, 1: 2, 2: 3, 6: 4, 9: 5, 11: 6, 13: 7}
-GATHERED = {1: 1, 5: 2, 8: 3, 12: 4, 14: 5, 16: 6, 18: 7}
+SPREAD = {-4: 1, -1: 2, 2: 3, 6: 4, 9: 5, 11: 6, 13: 7}
+GATHERED = {1: 1, 5: 2, 9: 3, 13: 4, 15: 5, 17: 6, 19: 7}
 WAIT_M = {20: (0, 2), 26: (2, 3)}
 WAIT_P = {21: (0, 2), 26: (2, 3)}
 TURN = {9: (0, 0, 2), 19: (0, 2, 4), 20: (1, 0, 2), 26: (1, 2, 3), 33: (1, 3, 4)}
@@ -184,29 +184,54 @@
         early = j < 16
         return jnp.where(early, j // 2 % 2, j // 8), jnp.where(early, j // 4, j // 2 % 4)
 
-    def piece(block, j):
+    def piece(block, j, two):
         quarter, w = place(j)
-        return blk.at[block, quarter, j % 2, pl.ds(pl.multiple_of(w * 256, 256), 256), :]
+        return blk.at[block, quarter, slice(None) if two else j % 2, pl.ds(pl.multiple_of(w * 256, 256), 256), :]
+
+    def z_sem(j, two):
+        return z_recv.at[SINGLE // 2 + j // 2 if two else j]
 
     def wait_bytes(ref, sem):
         pltpu.make_async_copy(ref, ref, sem).wait()
 
-    def send_z(j):
+    def send_z(j, two):
         pltpu.make_async_remote_copy(
-            src_ref=piece(OWN, j), dst_ref=piece(UP4, j),
-            send_sem=z_send, recv_sem=z_recv.at[j], device_id=at(-1, 0), device_id_type=MESH).start()
-
-    def send_m(block, j):
+            src_ref=piece(OWN, j, two), dst_ref=piece(UP4, j, two),
+            send_sem=z_send, recv_sem=z_sem(j, two), device_id=at(-1, 0), device_id_type=MESH).start()
+
+    def send_m(block, j, two):
         quarter, w = place(j)
         pltpu.make_async_remote_copy(
-            src_ref=piece(block, j), dst_ref=piece(UP1, j),
+            src_ref=piece(block, j, two), dst_ref=piece(UP1, j, two),
             send_sem=m_send, recv_sem=m_recv.at[quarter * 4 + w], device_id=at(0, -1), device_id_type=MESH).start()
 
-    def send_p(block, j):
+    def send_p(block, j, two):
         quarter, _ = place(j)
         pltpu.make_async_remote_copy(
-            src_ref=piece(block, j), dst_ref=piece(UP3, j),
+            src_ref=piece(block, j, two), dst_ref=piece(UP3, j, two),
             send_sem=p_send, recv_sem=p_recv.at[quarter], device_id=at(0, 1), device_id_type=MESH).start()
+
+    def send_on(j, two):
+        wait_bytes(piece(UP4, j, two), z_sem(j, two))
+
+        @pl.when((x <= 2) & (j < 24))
+        def _():
+            send_p(UP4, j, two)
+
+        @pl.when(x == 0)
+        def _():
+            send_m(UP4, j, two)
+
+    def send_own(j, two):
+        send_z(j, two)
+
+        @pl.when(x >= 1)
+        def _():
+            send_m(OWN, j, two)
+
+        @pl.when((x == 3) & (j < 24))
+        def _():
+            send_p(OWN, j, two)
 
     def turn(left, quarter):
         block = jnp.where(left == 0, OWN, UP1)
@@ -309,41 +334,26 @@
     def _(step):
         k = step + FIRST_STEP
 
-        @pl.when((k >= 0) & (k < PIECES))
-        def _():
-            wait_bytes(piece(UP4, k), z_recv.at[k])
-
-            @pl.when((x <= 2) & (k < 24))
-            def _():
-                send_p(UP4, k)
-
-            @pl.when(x == 0)
-            def _():
-                send_m(UP4, k)
-
-        @pl.when((k >= -4) & (k < 0))
+        @pl.when((k >= 0) & (k < SINGLE))
+        def _():
+            send_on(k, False)
+
+        @pl.when((k >= SINGLE) & (k < PIECES) & (k % 2 == 1))
+        def _():
+            send_on(k, True)
+
+        @pl.when((k >= -SINGLE) & (k < 0))
         def _():
             wait_bytes(wh.at[0, pl.ds(0, WIN - 1), 0, 0], aa_recv.at[FIRST + 4 + k])
+            send_own(k + SINGLE, False)
 
         @when_in(k, GATHERED)
         def _(sc):
             wait_bytes(wh.at[sc, pl.ds(0, WIN - 1)], aa_recv.at[sc])
 
-        lo = jnp.where(k < 0, k + 4, k + AHEAD + jnp.where(k > MORE_AHEAD, 1, 0))
-        count = jnp.where((k >= -4) & (k != 0) & (lo < PIECES), jnp.where(k == MORE_AHEAD, 2, 1), 0)
-        hi = lo + count
-
-        @pl.loop(lo, hi)
-        def _(j):
-            send_z(j)
-
-            @pl.when(x >= 1)
-            def _():
-                send_m(OWN, j)
-
-            @pl.when((x == 3) & (j < 24))
-            def _():
-                send_p(OWN, j)
+        @pl.when((k >= 0) & (k + AHEAD < PIECES) & (k % 2 == 1))
+        def _():
+            send_own(k + AHEAD, True)
 
         @when_in(k, FORWARD)
         def _(first, last):
@@ -458,7 +468,7 @@
             pltpu.VMEM((4, 2, ST, Q), BF16),
             pltpu.VMEM((SLOTS, 2, ST, ST), BF16),
             pltpu.VMEM((2, ST, 2 * Q), F32),
-            dma((4,)), dma((4,)), dma((4,)), dma((SLOTS_IN,)), dma((8,)), dma((FIRST + 4,)), dma, dma((PIECES,)), dma, dma((16,)), dma, dma((3,)),
+            dma((4,)), dma((4,)), dma((4,)), dma((SLOTS_IN,)), dma((8,)), dma((FIRST + 4,)), dma, dma(((SINGLE + PIECES) // 2,)), dma, dma((16,)), dma, dma((3,)),
             dma, dma((4,)), dma((5,)), dma((5,)), dma, dma,
         ],
         compiler_params=pltpu.CompilerParams(

time: 78.7 us -> 78.4 us (level)
  no operation moved by 1% of the time
where the time goes in v4:
time: 78.4 us; the launch traced here: 78.3 us
  Pallas kernels  76 us (97%)
  local copies, waits for them, and re-layouts  2.36 us (3%)
    pallas_call x1, Pallas kernels, shards(): pl.pallas_call(kernel, out_shape=jax.ShapeDtypeStruct((SLOTS, 2, ST, ST),...  76 us
    unnamed x1, local copies, waits for them, and re-layouts  2.36 us

profile of v4, /device:TPU:6, one launch (start us, length us, event | category | flops | bytes accessed | tf_op | source)
XLA Modules:
  0.0 78.3 jit_solution(13452104748803488659)
XLA Ops:
  0.0 76.0 %shard_map.37 = bf16[5,2,512,512]{3,2,1,0:T(8,128)(2,1)S(1)} custom-call(s32[1,5]{1,0:T(1,128)} %active_in.1, bf16[4,512,4096]{2,1,0:T(8,128)(2,1)} %rec.1, bf16[512,2048]{1,0:T(8,128)(2,1)} %constant.2.clone.table), custom_call_target="tpu_custom_call" | custom-call | flops 21474836480 | bytes 26214400 | tf_op jit(solution)/shard_map/pallas_call | solution.py:451
  76.0 2.4 %copy.6 = bf16[1,5,1,1024,512]{4,3,2,1,0:T(8,128)(2,1)} copy(bf16[1,5,1,1024,512]{4,3,2,1,0:T(8,128)(2,1)S(1)} %bitcast.3) | data formatting | bytes 10485760

commit v5 on v4

--- a/solution.py
+++ b/solution.py
@@ -50,7 +50,8 @@
 
 FIRST_STEP, LAST_STEP = -5, 43
 HALF = SAMPLES // 2
-PART_COLS = HALF // 4
+PARTS = 2
+PART_COLS = HALF // PARTS
 SINGLE = 4
 AHEAD = 4
 FIRST = 8
@@ -63,16 +64,16 @@
 BACK_HALF = {21: 0}
 BACK_TALL = {27: 2, 31: 3}
 BACK_WIDE = {26: (2, 0), 33: (3, 0), 34: (3, 1)}
-RETURN = {24: (0,), 27: (1, 2), 31: (3,), 34: (4,)}
+RETURN = {24: (0,), 27: (1, 2), 31: (3,), 33: (4,), 34: (5,)}
 RETURN_EARLY = 21
 SUMMARY = {10: (0, 0, 0), 16: (4, 0, 0), 22: (1, 0, 0), 23: (3, 0, 0), 24: (0, 0, 1), 25: (0, 1, 0), 28: (0, 1, 1),
            29: (4, 1, 0), 30: (3, 1, 0), 32: (1, 1, 0), 35: (4, 0, 1), 36: (4, 1, 1), 37: (1, 0, 1), 38: (1, 1, 1)}
 PART = {39: 0, 40: 1, 41: 2, 42: 3}
 FORWARD = {33: (0, 4)}
-TAKE = {31: (0,), 39: (1, 2), 41: (3,), 43: (4,)}
+TAKE = {31: (0,), 39: (1, 2), 41: (3,), 43: (4, 5)}
 TILE_AT = [(0, 0), (0, 1), (1, 0), (1, 1), (0, 2), (1, 2), (2, 2), (2, 0), (2, 1),
            (0, 3), (1, 3), (2, 3), (3, 0), (3, 1), (3, 2), (3, 3)]
-TILES_OF = [(0, 4), (4, 7), (7, 9), (9, 12), (12, 16)]
+TILES_OF = [(0, 4), (4, 7), (7, 9), (9, 12), (12, 14), (14, 16)]
 
 
 def kernel(active_in, rec, table, out, active, tab, rbuf, wh, blk, lt, rp, rv, ost, acc,
@@ -104,7 +105,7 @@
                 pltpu.make_async_copy(rec.at[0, pl.ds(0, 2 * Q), cols], rbuf.at[0, :, cols], first_sem.at[part]),
                 pltpu.make_async_copy(rec.at[0, pl.ds(0, 2 * Q), later], rbuf.at[0, :, later], later_sem.at[part]))
 
-    for part in range(4):
+    for part in range(PARTS):
         for copy in fetch(part):
             copy.start()
     flags = pltpu.make_async_copy(active_in, active, active_sem)
@@ -127,7 +128,7 @@
     def first_transform():
         acc[...] = jnp.zeros_like(acc)
 
-        @pl.loop(0, 4)
+        @pl.loop(0, PARTS)
         def _(part):
             for copy in fetch(part):
                 copy.wait()
@@ -288,7 +289,8 @@
             (pl.ds(2, 1), slice(None), pl.ds(0, 384)),
             (pl.ds(0, 2), slice(None), pl.ds(256, 128)),
             (pl.ds(3, 1), slice(None), pl.ds(0, 384)),
-            (pl.ds(0, 4), slice(None), pl.ds(384, 128)),
+            (pl.ds(0, 2), slice(None), pl.ds(384, 128)),
+            (pl.ds(2, 2), slice(None), pl.ds(384, 128)),
         ][n]
         return pltpu.make_async_remote_copy(
             src_ref=rp.at[sl], dst_ref=rv.at[sl],
@@ -435,7 +437,7 @@
             def _(n):
                 take_back(n)
 
-    for n in range(5):
+    for n in range(6):
         ret_copy(n).wait_send()
     wait_bytes(blk.at[UP3, 3], a2_send)
     wait_bytes(blk.at[OWN], z_send)
@@ -468,8 +470,8 @@
             pltpu.VMEM((4, 2, ST, Q), BF16),
             pltpu.VMEM((SLOTS, 2, ST, ST), BF16),
             pltpu.VMEM((2, ST, 2 * Q), F32),
-            dma((4,)), dma((4,)), dma((4,)), dma((SLOTS_IN,)), dma((8,)), dma((FIRST + 4,)), dma, dma(((SINGLE + PIECES) // 2,)), dma, dma((16,)), dma, dma((3,)),
-            dma, dma((4,)), dma((5,)), dma((5,)), dma, dma,
+            dma((PARTS,)), dma((PARTS,)), dma((PARTS,)), dma((SLOTS_IN,)), dma((8,)), dma((FIRST + 4,)), dma, dma(((SINGLE + PIECES) // 2,)), dma, dma((16,)), dma, dma((3,)),
+            dma, dma((4,)), dma((6,)), dma((6,)), dma, dma,
         ],
         compiler_params=pltpu.CompilerParams(
             collective_id=0, has_side_effects=True, vmem_limit_bytes=42 * 2**20),

time: 78.4 us -> 78.1 us (level)
  no operation moved by 1% of the time
where the time goes in v5:
time: 78.1 us; the launch traced here: 78 us
  Pallas kernels  75.6 us (97%)
  local copies, waits for them, and re-layouts  2.36 us (3%)
    pallas_call x1, Pallas kernels, shards(): pl.pallas_call(kernel, out_shape=jax.ShapeDtypeStruct((SLOTS, 2, ST, ST),...  75.6 us
    unnamed x1, local copies, waits for them, and re-layouts  2.36 us

profile of v5, /device:TPU:6, one launch (start us, length us, event | category | flops | bytes accessed | tf_op | source)
XLA Modules:
  0.0 78.0 jit_solution(98368577254146558)
XLA Ops:
  0.0 75.6 %shard_map.37 = bf16[5,2,512,512]{3,2,1,0:T(8,128)(2,1)S(1)} custom-call(s32[1,5]{1,0:T(1,128)} %active_in.1, bf16[4,512,4096]{2,1,0:T(8,128)(2,1)} %rec.1, bf16[512,2048]{1,0:T(8,128)(2,1)} %constant.2.clone.table), custom_call_target="tpu_custom_call" | custom-call | flops 21474836480 | bytes 26214400 | tf_op jit(solution)/shard_map/pallas_call | solution.py:453
  75.7 2.4 %copy.6 = bf16[1,5,1,1024,512]{4,3,2,1,0:T(8,128)(2,1)} copy(bf16[1,5,1,1024,512]{4,3,2,1,0:T(8,128)(2,1)S(1)} %bitcast.3) | data formatting | bytes 10485760

commit v6 on v5

--- a/solution.py
+++ b/solution.py
@@ -173,7 +173,7 @@
                 src = wh.at[sc, to[0], part // 2, part % 2]
                 dst = blk.at[OWN, part // 2, part % 2, pl.ds(row, BAND_BINS), :]
             pltpu.make_async_remote_copy(
-                src_ref=src, dst_ref=dst, send_sem=aa_send.at[sc],
+                src_ref=src, dst_ref=dst, send_sem=aa_send,
                 recv_sem=aa_recv.at[sc if part is None else FIRST + part],
                 device_id=to, device_id_type=MESH,
             ).start()
@@ -294,7 +294,7 @@
         ][n]
         return pltpu.make_async_remote_copy(
             src_ref=rp.at[sl], dst_ref=rv.at[sl],
-            send_sem=ret_send.at[n], recv_sem=ret_recv.at[n], device_id=nxt, device_id_type=MESH)
+            send_sem=ret_send, recv_sem=ret_recv.at[n], device_id=nxt, device_id_type=MESH)
 
     def give_back(rows, quarters):
         parts = [[blk[jnp.where(c == 3, UP4, UP3), c, ri] for c in quarters] for ri in range(2)]
@@ -357,7 +357,7 @@
         def _():
             send_own(k + AHEAD, True)
 
-        @when_in(k, FORWARD)
+        @when_in(jnp.where((x == 1) | (x == 2), k + 2, k), FORWARD)
         def _(first, last):
             @pl.loop(first, last)
             def _(w):
@@ -437,14 +437,12 @@
             def _(n):
                 take_back(n)
 
-    for n in range(6):
-        ret_copy(n).wait_send()
+    wait_bytes(rp, ret_send)
     wait_bytes(blk.at[UP3, 3], a2_send)
     wait_bytes(blk.at[OWN], z_send)
     wait_bytes(blk.at[OWN], m_send)
     wait_bytes(blk.at[OWN, pl.ds(0, 3)], p_send)
-    for sc in range(8):
-        wait_bytes(wh.at[sc, pl.ds(0, WIN - 1)], aa_send.at[sc])
+    wait_bytes(wh.at[:, pl.ds(0, WIN - 1)], aa_send)
     pltpu.make_async_copy(ost, out, out_sem).wait()
 
 
@@ -470,8 +468,8 @@
             pltpu.VMEM((4, 2, ST, Q), BF16),
             pltpu.VMEM((SLOTS, 2, ST, ST), BF16),
             pltpu.VMEM((2, ST, 2 * Q), F32),
-            dma((PARTS,)), dma((PARTS,)), dma((PARTS,)), dma((SLOTS_IN,)), dma((8,)), dma((FIRST + 4,)), dma, dma(((SINGLE + PIECES) // 2,)), dma, dma((16,)), dma, dma((3,)),
-            dma, dma((4,)), dma((6,)), dma((6,)), dma, dma,
+            dma((PARTS,)), dma((PARTS,)), dma((PARTS,)), dma((SLOTS_IN,)), dma, dma((FIRST + 4,)), dma, dma(((SINGLE + PIECES) // 2,)), dma, dma((16,)), dma, dma((3,)),
+            dma, dma((4,)), dma, dma((6,)), dma, dma,
         ],
         compiler_params=pltpu.CompilerParams(
             collective_id=0, has_side_effects=True, vmem_limit_bytes=42 * 2**20),

time: 78.1 us -> 78 us (level)
  no operation moved by 1% of the time
where the time goes in v6:
time: 78 us; the launch traced here: 77.9 us
  Pallas kernels  75.5 us (97%)
  local copies, waits for them, and re-layouts  2.36 us (3%)
    pallas_call x1, Pallas kernels, shards(): pl.pallas_call(kernel, out_shape=jax.ShapeDtypeStruct((SLOTS, 2, ST, ST),...  75.5 us
    unnamed x1, local copies, waits for them, and re-layouts  2.36 us

profile of v6, /device:TPU:6, one launch (start us, length us, event | category | flops | bytes accessed | tf_op | source)
XLA Modules:
  0.0 77.9 jit_solution(9745221467432754600)
XLA Ops:
  0.0 75.5 %shard_map.37 = bf16[5,2,512,512]{3,2,1,0:T(8,128)(2,1)S(1)} custom-call(s32[1,5]{1,0:T(1,128)} %active_in.1, bf16[4,512,4096]{2,1,0:T(8,128)(2,1)} %rec.1, bf16[512,2048]{1,0:T(8,128)(2,1)} %constant.2.clone.table), custom_call_target="tpu_custom_call" | custom-call | flops 21474836480 | bytes 26214400 | tf_op jit(solution)/shard_map/pallas_call | solution.py:451
  75.5 2.4 %copy.6 = bf16[1,5,1,1024,512]{4,3,2,1,0:T(8,128)(2,1)} copy(bf16[1,5,1,1024,512]{4,3,2,1,0:T(8,128)(2,1)S(1)} %bitcast.3) | data formatting | bytes 10485760
